TPU v7x, 32 devices: a whole 2x2x4 slice. The times are simulated.
32 devices in a mesh: lm: 8 (over y, x, core), kf: 4 (over z).
Axes of the slice: x: 2, y: 2, z: 4, core: 2. Of those that a mesh axis runs over, the one named last changes fastest.
Arguments:
- land_rhs: float32 [3, 131072], P(None, ('lm', 'kf')), may hold values from -6 to 6
- key_rhs: float32 [15, 16384], P(None, ('lm', 'kf')), may hold values from -6 to 6
- land_damp: float32 [3, 131072], P(None, ('lm', 'kf')), may hold values from 0.5 to 2
- key_damp: float32 [15, 16384], P(None, ('lm', 'kf')), may hold values from 0.5 to 2
- land_jac: float32 [6, 524288], P(None, ('lm', 'kf')), may hold values from -4 to 4
- key_jac: float32 [30, 524288], P(None, ('lm', 'kf')), may hold values from -1.5 to 1.5
- obs_landmark: int32 [524288], P(('lm', 'kf')), may hold values from 0 to 16383, as said below
- obs_keyframe: int32 [524288], P(('lm', 'kf')), may hold values from 0 to 16383, as said below
- live_blocks: int32 [32], P(('lm', 'kf')), may hold values from 32 to 128, as said below
- preint: float32 [240, 245760], P(None, ('lm', 'kf')), as said below
Outputs:
- sol_land: float32 [3, 131072], P(None, ('lm', 'kf'))
- sol_key: float32 [15, 16384], P(None, ('lm', 'kf'))
Inputs may be any that keep to these rules, and one draw needn't show every extreme that they name: `obs_landmark`: offsets among the 16384 landmarks of the lm index of the device holding the row. `obs_keyframe`: row o names a state s whose device index (s // 512) has the same kf index as the device holding row o. `live_blocks`: blocks past a device's count are padding; some device uses all its blocks. `preint`: each window's block is symmetric, and its diagonal exceeds the sum of magnitudes off the diagonal in its row.
All inputs are finite; a program needn't handle non-finite values.
Results may differ from a plain program's by a relative error of at most 0.0001.
Values sent between devices are 32-bit elements; how exact they have to be, the bound alone decides.
A program may use at most 128 MiB of HBM per device.

v0:
```python
import jax
import jax.numpy as jnp
from jax import lax
from jax.sharding import PartitionSpec as P

WSTATES = 16
SDIM = 15
BLOCK = 128
ITERS = 2
WPAR = 240


def window_product(preint, vectors):
    windows = preint.shape[1] // WPAR
    blocks = preint.reshape(WPAR, windows, WPAR)
    stacked = vectors.reshape(SDIM, windows, WSTATES).transpose(1, 2, 0).reshape(windows, WPAR)
    mapped = jnp.einsum("awb,wb->wa", blocks, stacked, precision=lax.Precision.HIGHEST)
    return (
        mapped.reshape(windows, WSTATES, SDIM).transpose(2, 0, 1).reshape(SDIM, windows * WSTATES)
    )


def split_tables(positions, extent):
    low_width = 128
    high_count = extent // low_width
    low_hot = (
        positions[None, :] % low_width == jnp.arange(low_width, dtype=jnp.int32)[:, None]
    ).astype(jnp.float32)
    high_hot = (
        positions[None, :] // low_width == jnp.arange(high_count, dtype=jnp.int32)[:, None]
    ).astype(jnp.float32)
    return (low_hot, high_hot)


def pick_columns(table, low_hot, high_hot):
    channels = table.shape[0]
    high_count = high_hot.shape[0]
    low_width = low_hot.shape[0]
    spans = low_hot.shape[1]
    folded = table.reshape(channels * high_count, low_width)
    partial_rows = jnp.dot(
        folded, low_hot, precision=lax.Precision.HIGHEST, preferred_element_type=jnp.float32
    )
    return jnp.sum(partial_rows.reshape(channels, high_count, spans) * high_hot[None], axis=1)


def spread_columns(values, low_hot, high_hot):
    channels = values.shape[0]
    high_count = high_hot.shape[0]
    low_width = low_hot.shape[0]
    spans = low_hot.shape[1]
    placed = (values[:, None, :] * high_hot[None]).reshape(channels * high_count, spans)
    summed = lax.dot_general(
        placed,
        low_hot,
        (((1,), (1,)), ((), ())),
        precision=lax.Precision.HIGHEST,
        preferred_element_type=jnp.float32,
    )
    return summed.reshape(channels, high_count * low_width)


def observe(land_jac, key_jac, land_pos, key_pos, live, land_full, key_full):
    span = 16 * BLOCK
    turns = (live + 15) // 16
    limit = live * BLOCK
    land_extent = land_full.shape[1]
    key_extent = key_full.shape[1]

    def one_turn(turn_index, carry):
        summed_land, summed_key = carry
        start = turn_index * span
        land_rows = lax.dynamic_slice_in_dim(land_jac, start, span, 1).reshape(2, 3, span)
        key_rows = lax.dynamic_slice_in_dim(key_jac, start, span, 1).reshape(2, SDIM, span)
        land_index = lax.dynamic_slice_in_dim(land_pos, start, span, 0)
        key_index = lax.dynamic_slice_in_dim(key_pos, start, span, 0)
        inside = (start + jnp.arange(span, dtype=jnp.int32) < limit).astype(jnp.float32)
        land_low, land_high = split_tables(land_index, land_extent)
        key_low, key_high = split_tables(key_index, key_extent)
        seen_land = pick_columns(land_full, land_low, land_high)
        seen_key = pick_columns(key_full, key_low, key_high)
        image = jnp.sum(land_rows * seen_land[None], axis=1) + jnp.sum(
            key_rows * seen_key[None], axis=1
        )
        image = image * inside[None]
        back_land = jnp.sum(land_rows * image[:, None], axis=0)
        back_key = jnp.sum(key_rows * image[:, None], axis=0)
        return (
            summed_land + spread_columns(back_land, land_low, land_high),
            summed_key + spread_columns(back_key, key_low, key_high),
        )

    start_carry = (jnp.zeros_like(land_full), jnp.zeros_like(key_full))
    return lax.fori_loop(0, turns, one_turn, start_carry)


def shards(
    land_rhs,
    key_rhs,
    land_damp,
    key_damp,
    land_jac,
    key_jac,
    obs_landmark,
    obs_keyframe,
    live_blocks,
    preint,
):
    state_dev = key_rhs.shape[1]
    kf_count = lax.axis_size("kf")
    lm_place = lax.axis_index("lm")
    owner_block = obs_keyframe // state_dev
    key_pos = owner_block // kf_count * state_dev + obs_keyframe % state_dev
    live = live_blocks[0]
    own_start = lm_place * state_dev

    def own_part(vector):
        return lax.dynamic_slice_in_dim(vector, own_start, state_dev, 1)

    def inner_sum(left_land, right_land, left_key, right_key):
        return jnp.sum(left_land * right_land) + jnp.sum(own_part(left_key) * own_part(right_key))

    res_key = lax.all_gather(key_rhs, "lm", axis=1, tiled=True)
    res_land = land_rhs
    sol_land = jnp.zeros_like(res_land)
    sol_key = jnp.zeros_like(res_key)

    def squares(part_land, part_key):
        return lax.psum(inner_sum(part_land, part_land, part_key, part_key), ("lm", "kf"))

    dir_land, dir_key = (res_land, res_key)
    norm_now = squares(res_land, res_key)
    for iteration in range(ITERS):
        land_full = lax.all_gather(dir_land, "kf", axis=1, tiled=True)
        key_full = dir_key
        summed_land, summed_key = observe(
            land_jac, key_jac, obs_landmark, key_pos, live, land_full, key_full
        )
        prod_land = (
            lax.psum_scatter(summed_land, "kf", scatter_dimension=1, tiled=True)
            + land_damp * dir_land
        )
        own_dir = own_part(dir_key)
        local_terms = key_damp * own_dir + window_product(preint, own_dir)
        placed = lax.dynamic_update_slice_in_dim(
            jnp.zeros_like(summed_key), local_terms, own_start, 1
        )
        prod_key = lax.psum(summed_key + placed, "lm")
        prod_land, prod_key = (prod_land, prod_key)
        step_size = norm_now / lax.psum(
            inner_sum(dir_land, prod_land, dir_key, prod_key), ("lm", "kf")
        )
        sol_land = sol_land + step_size * dir_land
        sol_key = sol_key + step_size * dir_key
        res_land = res_land - step_size * prod_land
        res_key = res_key - step_size * prod_key
        norm_next = squares(res_land, res_key)
        dir_land = res_land + norm_next / norm_now * dir_land
        dir_key = res_key + norm_next / norm_now * dir_key
        norm_now = norm_next
    return (sol_land, own_part(sol_key))


def solution(mesh):
    in_specs = (
        P(None, ("lm", "kf")),
        P(None, ("lm", "kf")),
        P(None, ("lm", "kf")),
        P(None, ("lm", "kf")),
        P(None, ("lm", "kf")),
        P(None, ("lm", "kf")),
        P(("lm", "kf")),
        P(("lm", "kf")),
        P(("lm", "kf")),
        P(None, ("lm", "kf")),
    )
    out_specs = (P(None, ("lm", "kf")), P(None, ("lm", "kf")))
    return jax.shard_map(shards, mesh=mesh, in_specs=in_specs, out_specs=out_specs, check_vma=False)
```

profile of v0, /device:TPU:0, one launch (start us, length us, event | category | flops | bytes accessed | tf_op | source)
XLA Modules:
  0.0 729.1 jit_solution(2431009380259834372)
XLA Ops:
  8.7 11.0 %all_gather.9 = f32[15,4096]{1,0:T(8,128)S(1)} all-gather(f32[15,512]{1,0:T(8,128)} %param.15), channel_id=1, replica_groups=mesh['lm'=8,'kf'=4] {'lm'}, dimensions={1}, use_global_device_ids=true | all-gather | bytes 276480 | tf_op jit(solution)/shard_map/all_gather | solution.py:123
  19.8 14.3 %all_gather.10 = f32[3,16384]{1,0:T(4,128)S(1)} all-gather(f32[3,4096]{1,0:T(4,128)} %param.14), channel_id=1, replica_groups=mesh['lm'=8,'kf'=4] {'kf'}, dimensions={1}, use_global_device_ids=true | all-gather | bytes 245760 | tf_op jit(solution)/shard_map/all_gather | solution.py:134
  35.3 77.5 %while.40 = (s32[]{:T(128)}, f32[3,16384]{1,0:T(4,128)S(1)}, f32[15,4096]{1,0:T(8,128)S(1)}, s32[]{:T(128)}, f32[6,16384]{1,0:T(8,128)}, /*index=5*/s32[16384]{0...) while((s32[]{:T(128)}, f32[3,16384]{1,0:T(4,128)S(1)}, ...), condition=%wide.wide.region_10.11_spmd, body=%wide.wide.region_3.10_spmd.sunk | while | flops 5443270656 | bytes 37953768 | solution.py:94
  36.1 1.7 fusion.90
  43.8 2.0 fusion.94
  49.0 1.7 fusion.90
  56.7 2.0 fusion.94
  59.2 1.7 fusion.93
  61.8 1.7 fusion.90
  69.6 2.0 fusion.94
  72.1 1.7 fusion.93
  74.7 1.7 fusion.90
  82.4 2.0 fusion.94
  87.6 1.7 fusion.90
  95.3 2.0 fusion.94
  100.5 1.7 fusion.90
  108.2 2.0 fusion.94
  114.1 11.4 %reshape.446 = f32[240,32,240]{2,1,0:T(8,128)} reshape(f32[240,7680]{1,0:T(8,128)} %param.23) | data formatting | bytes 14745600 | tf_op jit(solution)/shard_map/reshape | solution.py:15
  125.6 4.4 multiply_reduce_fusion.13
  131.1 5.1 copy.30
  136.3 74.7 %all-reduce.4.cloned.1.call-done = f32[15,4096]{1,0:T(8,128)} async-done(((f32[15,4096]{1,0:T(8,128)}), f32[15,4096]{1,0:T(8,128)}) %all-reduce.4.cloned.1.call-update) | async-done | bytes 245776 | tf_op jit(solution)/shard_map/psum | solution.py:148
  212.4 94.6 %reduce-scatter.7.cloned.1.call-done = f32[4096,3]{1,0:T(8,128)} async-done(((f32[16384,3]{1,0:T(8,128)}), f32[4096,3]{1,0:T(8,128)}) %reduce-scatter.7.cloned.1.call-update) | async-done | bytes 49168
  307.0 2.2 copy.31
  312.4 40.9 %all-reduce = (f32[]{:T(128)}, f32[]{:T(128)}) all-reduce(f32[]{:T(128)S(6)} %add.269, f32[]{:T(128)S(6)} %add.277), channel_id=1, replica_groups=mesh['lm'=8,'kf'=4] {'lm','kf'}, use_global_device_ids=true, to_apply=%region_2.3 | all-reduce | flops 2 | bytes 16 | tf_op jit(solution)/shard_map/psum | solution.py:129
  358.3 39.3 %psum.45 = f32[]{:T(128)} all-reduce(f32[]{:T(128)S(6)} %add.278), channel_id=1, replica_groups=mesh['lm'=8,'kf'=4] {'lm','kf'}, use_global_device_ids=true, to_apply=%region_18.19 | all-reduce | flops 1 | bytes 8 | tf_op jit(solution)/shard_map/psum | solution.py:129
  399.6 4.3 multiply_reduce_fusion.12
  404.3 14.2 %all_gather.11 = f32[3,16384]{1,0:T(4,128)S(1)} all-gather(f32[3,4096]{1,0:T(4,128)S(1)} %multiply_add_fusion.2), channel_id=1, replica_groups=mesh['lm'=8,'kf'=4] {'kf'}, dimensions={1}, use_global_device_ids=true | all-gather | bytes 245760 | tf_op jit(solution)/shard_map/all_gather | solution.py:134
  419.2 77.1 %while.41 = (s32[]{:T(128)}, f32[3,16384]{1,0:T(4,128)S(1)}, f32[15,4096]{1,0:T(8,128)S(1)}, s32[]{:T(128)}, f32[6,16384]{1,0:T(8,128)}, /*index=5*/s32[16384]{0...) while((s32[]{:T(128)}, f32[3,16384]{1,0:T(4,128)S(1)}, ...), condition=%wide.wide.region_26.27_spmd, body=%wide.wide.region_19.26_spmd.sunk | while | flops 5443270656 | bytes 37953768 | solution.py:94
  419.9 1.7 fusion.101
  427.6 2.0 fusion.105
  432.8 1.7 fusion.101
  440.5 2.0 fusion.105
  443.0 1.7 fusion.104
  445.7 1.7 fusion.101
  453.4 2.0 fusion.105
  455.9 1.7 fusion.104
  458.5 1.7 fusion.101
  466.2 2.0 fusion.105
  471.4 1.7 fusion.101
  479.1 2.0 fusion.105
  484.2 1.7 fusion.101
  491.9 2.0 fusion.105
  494.5 1.7 fusion.104
  497.9 5.1 copy.32
  503.0 74.3 %all-reduce.6.cloned.1.call-done = f32[15,4096]{1,0:T(8,128)} async-done(((f32[15,4096]{1,0:T(8,128)}), f32[15,4096]{1,0:T(8,128)}) %all-reduce.6.cloned.1.call-update) | async-done | bytes 245776 | tf_op jit(solution)/shard_map/psum | solution.py:148
  578.7 94.6 %reduce-scatter.9.cloned.1.call-done = f32[4096,3]{1,0:T(8,128)} async-done(((f32[16384,3]{1,0:T(8,128)}), f32[4096,3]{1,0:T(8,128)}) %reduce-scatter.9.cloned.1.call-update) | async-done | bytes 49168
  673.3 2.2 copy.33
  677.5 40.9 %psum.47 = f32[]{:T(128)} all-reduce(f32[]{:T(128)S(6)} %add.284), channel_id=1, replica_groups=mesh['lm'=8,'kf'=4] {'lm','kf'}, use_global_device_ids=true, to_apply=%region_31.32 | all-reduce | flops 1 | bytes 8 | tf_op jit(solution)/shard_map/psum | solution.py:150
  (359 shorter events, 114.7 us)
Async XLA Ops:
  8.0 203.0 %all-reduce.4.cloned.1.call-start = ((), (), s32[]{:S(2)}) async-start(), calls=%async_computation.2 | async-start | bytes 524288 | tf_op jit(solution)/shard_map/psum | solution.py:148
  19.7 15.6 %copy-start.2 = (f32[15,4096]{1,0:T(8,128)}, f32[15,4096]{1,0:T(8,128)S(1)}, u32[]{:S(2)}) copy-start(f32[15,4096]{1,0:T(8,128)S(1)} %all_gather.9) | copy-start | bytes 737284
  34.1 1.2 copy-start.6
  125.6 4.7 copy-start.3
  125.6 4.7 copy-start.9
  130.3 0.7 copy-start.1
  131.0 176.0 %reduce-scatter.7.cloned.1.call-start = ((), (), s32[]{:S(2)}) async-start(), calls=%async_computation.4 | async-start | bytes 10485760
  136.2 173.0 %copy-start.4 = (f32[3,4096]{1,0:T(4,128)S(1)}, f32[3,4096]{1,0:T(4,128)}, u32[]{:S(2)}) copy-start(f32[3,4096]{1,0:T(4,128)} %param.14) | copy-start | bytes 147460
  136.2 173.0 %copy-start.8 = (f32[3,4096]{1,0:T(4,128)S(1)}, f32[3,4096]{1,0:T(4,128)}, u32[]{:S(2)}) copy-start(f32[3,4096]{1,0:T(4,128)} %param.16) | copy-start | bytes 147460
  136.2 441.1 %all-reduce.6.cloned.1.call-start = ((), (), s32[]{:S(2)}) async-start(), calls=%async_computation.3 | async-start | bytes 524288 | tf_op jit(solution)/shard_map/psum | solution.py:148
  398.9 5.1 copy-start.5
  418.5 0.7 copy-start.7
  497.1 0.7 copy-start
  497.9 175.5 %reduce-scatter.9.cloned.1.call-start = ((), (), s32[]{:S(2)}) async-start(), calls=%async_computation.5 | async-start | bytes 10485760
Sparse Core Ops, SparseCore 0:
  131.2 79.7 all-reduce.3
  498.0 79.2 all-reduce.5
Sparse Core Ops, SparseCore 1:
  136.3 170.7 reduce-scatter.6
  503.1 170.2 reduce-scatter.8
where the time goes:
time: 733 us; the launch traced here: 729 us
  waiting for transfers between devices  338 us (46%)
  blocking collectives  161 us (22%)
  matrix products  81.8 us (11%)
  other arithmetic  65.7 us (9%)
  local copies, waits for them, and re-layouts  54.9 us (7%)
  between operations  25.4 us (3%)
    unnamed x6, waiting for transfers between devices  189 us
    psum x2, waiting for transfers between devices, shards(): prod_key = lax.psum(summed_key + placed, 'lm')  149 us
    psum x2, blocking collectives, squares(): lax.psum(inner_sum(part_land, part_land, part_key, part_key), ('lm', 'kf'))  80.2 us
    dot_general x24, matrix products, spread_columns(): lax.dot_general(placed, low_hot, (((1,), (1,)), ((), ())), precision=lax....  44.1 us
    psum x1, blocking collectives, shards(): lax.psum(inner_sum(dir_land, prod_land, dir_key, prod_key), ('lm', 'kf'))  40.9 us
    dot_general x24, matrix products, pick_columns(): jnp.dot(folded, low_hot, precision=lax.Precision.HIGHEST, preferred_eleme...  37.7 us
    all_gather x2, blocking collectives, shards(): land_full = lax.all_gather(dir_land, 'kf', axis=1, tiled=True)  28.6 us
    unnamed x28, local copies, waits for them, and re-layouts  17.3 us
  transfers between devices with their start and end apart: 4, of which 4 were waited for; matrix products, arithmetic and copies ran while one was open for 2% of the time, Pallas kernels for 0%

commit v1 on v0

v1 whole, which is shorter than its diff:
```python
import functools
import jax
import jax.numpy as jnp
from jax import lax
from jax.experimental import pallas as pl
from jax.experimental.pallas import tpu as pltpu
from jax.sharding import PartitionSpec as P

WSTATES = 16
SDIM = 15
BLOCK = 128
ITERS = 2
WPAR = 240
LOW = 256
CHUNK = 1024
F32 = jnp.float32
BF16 = jnp.bfloat16


def halves(value):
    high = value.astype(BF16).astype(F32)
    return high, value - high


def stacked_halves(value):
    high, low = halves(value)
    return jnp.concatenate([high.astype(BF16), low.astype(BF16)], axis=0)


def observe_kernel(
    live_ref, lt_ref, kt_ref, lj_ref, kj_ref, il_ref, ik_ref, ol_ref, ok_ref,
    lhl_ref, khl_ref, kjp_ref, lacc_ref, kacc_ref, lplace_ref, kplace_ref,
):
    land_rows = lt_ref.shape[0]
    key_rows = kt_ref.shape[0]
    groups = land_rows // 48
    highs = key_rows // 16
    total = il_ref.shape[1]
    span = CHUNK
    limit = live_ref[0] * BLOCK
    lhl_ref[...] = stacked_halves(lt_ref[...])
    khl_ref[...] = stacked_halves(kt_ref[...])
    lacc_ref[...] = jnp.zeros_like(lacc_ref)
    kacc_ref[...] = jnp.zeros_like(kacc_ref)
    kjp_ref[...] = jnp.zeros_like(kjp_ref)

    def turn(index, carry):
        start = pl.multiple_of(index * span, span)
        cols = pl.ds(start, span)
        kjp_ref[0:SDIM, :] = kj_ref[0:SDIM, cols]
        kjp_ref[16 : 16 + SDIM, :] = kj_ref[SDIM : 2 * SDIM, cols]
        lpos = il_ref[:, cols]
        kpos = ik_ref[:, cols]
        lhigh = lpos // LOW
        khigh = kpos // LOW
        low_iota = lax.broadcasted_iota(jnp.int32, (LOW, span), 0)
        lhot = jnp.where(low_iota == lpos % LOW, 1.0, 0.0).astype(BF16)
        khot = jnp.where(low_iota == kpos % LOW, 1.0, 0.0).astype(BF16)
        lall = jnp.dot(lhl_ref[...], lhot, preferred_element_type=F32)
        kall = jnp.dot(khl_ref[...], khot, preferred_element_type=F32)
        high_iota = lax.broadcasted_iota(jnp.int32, (16, span), 0)
        lmask = [lhigh - 16 * d == high_iota for d in range(groups)]
        kmask = [jnp.broadcast_to(khigh, (16, span)) == h for h in range(highs)]
        seen_land = []
        for c in range(3):
            part = jnp.zeros((16, span), F32)
            for d in range(groups):
                row = d * 48 + c * 16
                both = lall[row : row + 16] + lall[land_rows + row : land_rows + row + 16]
                part = jnp.where(lmask[d], both, part)
            seen_land.append(jnp.sum(part, axis=0, keepdims=True))
        seen_key = jnp.zeros((16, span), F32)
        for h in range(highs):
            both = kall[h * 16 : h * 16 + 16] + kall[key_rows + h * 16 : key_rows + h * 16 + 16]
            seen_key = jnp.where(kmask[h], both, seen_key)
        inside = start + lax.broadcasted_iota(jnp.int32, (1, span), 1) < limit
        image = []
        for r in range(2):
            value = jnp.sum(kjp_ref[r * 16 : r * 16 + 16, :] * seen_key, axis=0, keepdims=True)
            for c in range(3):
                value = value + lj_ref[r * 3 + c : r * 3 + c + 1, cols] * seen_land[c]
            image.append(jnp.where(inside, value, 0.0))
        for c in range(3):
            back = (
                lj_ref[c : c + 1, cols] * image[0] + lj_ref[3 + c : 4 + c, cols] * image[1]
            )
            for p, part in enumerate(halves(back)):
                part = jnp.broadcast_to(part, (16, span))
                for d in range(groups):
                    row = p * land_rows + d * 48 + c * 16
                    lplace_ref[row : row + 16, :] = jnp.where(lmask[d], part, 0.0).astype(BF16)
        back = kjp_ref[0:16, :] * image[0] + kjp_ref[16:32, :] * image[1]
        for p, part in enumerate(halves(back)):
            for h in range(highs):
                row = p * key_rows + h * 16
                kplace_ref[row : row + 16, :] = jnp.where(kmask[h], part, 0.0).astype(BF16)
        contract = (((1,), (1,)), ((), ()))
        lacc_ref[...] += lax.dot_general(
            lplace_ref[...], lhot, contract, preferred_element_type=F32
        )
        kacc_ref[...] += lax.dot_general(
            kplace_ref[...], khot, contract, preferred_element_type=F32
        )
        return carry

    lax.fori_loop(0, total // span, turn, 0)
    ol_ref[...] = lacc_ref[0:land_rows, :] + lacc_ref[land_rows:, :]
    ok_ref[...] = kacc_ref[0:key_rows, :] + kacc_ref[key_rows:, :]


def observe(live, land_table, key_table, land_jac, key_jac, land_pos, key_pos):
    land_rows, key_rows = land_table.shape[0], key_table.shape[0]
    vmem = pl.BlockSpec(memory_space=pltpu.VMEM)
    return pl.pallas_call(
        observe_kernel,
        out_shape=(
            jax.ShapeDtypeStruct((land_rows, LOW), F32),
            jax.ShapeDtypeStruct((key_rows, LOW), F32),
        ),
        in_specs=[pl.BlockSpec(memory_space=pltpu.SMEM)] + [vmem] * 6,
        out_specs=(vmem, vmem),
        scratch_shapes=[
            pltpu.VMEM((2 * land_rows, LOW), BF16),
            pltpu.VMEM((2 * key_rows, LOW), BF16),
            pltpu.VMEM((32, CHUNK), F32),
            pltpu.VMEM((2 * land_rows, LOW), F32),
            pltpu.VMEM((2 * key_rows, LOW), F32),
            pltpu.VMEM((2 * land_rows, CHUNK), BF16),
            pltpu.VMEM((2 * key_rows, CHUNK), BF16),
        ],
        compiler_params=pltpu.CompilerParams(vmem_limit_bytes=50 * 2**20),
    )(live, land_table, key_table, land_jac, key_jac, land_pos, key_pos)


def window_kernel(pre_ref, dir_ref, out_ref, ex_ref, y_ref):
    width = pre_ref.shape[1]
    windows = width // WPAR
    states = windows * WSTATES
    for t in range(WSTATES):
        for h in range(states // LOW):
            ex_ref[t * SDIM : (t + 1) * SDIM, h * LOW : (h + 1) * LOW] = dir_ref[
                h * 16 : h * 16 + SDIM, :
            ]
    rows = lax.broadcasted_iota(jnp.int32, (WPAR, states), 0)
    cols = lax.broadcasted_iota(jnp.int32, (WPAR, states), 1)
    own_time = rows // SDIM == cols % WSTATES
    group = jnp.where(
        lax.broadcasted_iota(jnp.int32, (windows, states), 1) // WSTATES
        == lax.broadcasted_iota(jnp.int32, (windows, states), 0),
        1.0,
        0.0,
    ).astype(BF16)
    placed = jnp.where(own_time, ex_ref[...], 0.0)
    parts = [
        lax.dot_general(
            group, part.astype(BF16), (((1,), (1,)), ((), ())), preferred_element_type=F32
        ).astype(BF16)
        for part in halves(placed)
    ]
    both = jnp.concatenate(parts, axis=0)
    step = 768
    for start in range(0, width, step):
        high, low = halves(pre_ref[:, start : start + step])
        first = jnp.dot(both, high.astype(BF16), preferred_element_type=F32)
        second = jnp.dot(parts[0], low.astype(BF16), preferred_element_type=F32)
        y_ref[:, start : start + step] = first[:windows] + first[windows:] + second
    y_ref[:, width:] = jnp.zeros((windows, y_ref.shape[1] - width), F32)
    own_row = lax.broadcasted_iota(jnp.int32, (8, LOW), 0)
    strips = []
    for tile in range(windows // 8):
        strip = jnp.zeros((8, LOW), F32)
        for r in range(8):
            begin = (tile * 8 + r) * WPAR
            base = begin // 128 * 128
            block = y_ref[tile * 8 : tile * 8 + 8, base : base + 384]
            if begin != base:
                block = pltpu.roll(block, 384 - (begin - base), 1)
            strip = jnp.where(own_row == r, block[:, :LOW], strip)
        strips.append(strip)
    mapped = jnp.concatenate(strips, axis=0).T[:WPAR]
    spread = jnp.zeros((WPAR, states), F32)
    for part in halves(mapped):
        spread = spread + jnp.dot(part.astype(BF16), group, preferred_element_type=F32)
    ex_ref[...] = jnp.where(own_time, spread, 0.0)
    result = ex_ref[0:SDIM, :]
    for t in range(1, WSTATES):
        result = result + ex_ref[t * SDIM : (t + 1) * SDIM, :]
    out_ref[...] = jnp.zeros_like(out_ref)
    for h in range(states // LOW):
        out_ref[h * 16 : h * 16 + SDIM, :] = result[:, h * LOW : (h + 1) * LOW]


def window_product(preint, direction):
    windows = preint.shape[1] // WPAR
    vmem = pl.BlockSpec(memory_space=pltpu.VMEM)
    return pl.pallas_call(
        window_kernel,
        out_shape=jax.ShapeDtypeStruct(direction.shape, F32),
        in_specs=[vmem, vmem],
        out_specs=vmem,
        scratch_shapes=[
            pltpu.VMEM((WPAR, windows * WSTATES), F32),
            pltpu.VMEM((windows, preint.shape[1] + 384), F32),
        ],
        compiler_params=pltpu.CompilerParams(vmem_limit_bytes=50 * 2**20),
    )(preint, direction)


def fold_key(array):
    states = array.shape[1]
    parts = array.reshape(SDIM, states // LOW, LOW).transpose(1, 0, 2)
    return jnp.pad(parts, ((0, 0), (0, 1), (0, 0))).reshape(-1, LOW)


def unfold_key(array):
    parts = array.reshape(-1, 16, LOW)[:, :SDIM].transpose(1, 0, 2)
    return parts.reshape(SDIM, -1)


def shards(
    land_rhs, key_rhs, land_damp, key_damp, land_jac, key_jac,
    obs_landmark, obs_keyframe, live_blocks, preint,
):
    state_dev = key_rhs.shape[1]
    kf_count = lax.axis_size("kf")
    key_pos = obs_keyframe // state_dev // kf_count * state_dev + obs_keyframe % state_dev
    key_pos = key_pos[None]
    land_pos = obs_landmark[None]
    land_shape = land_rhs.shape
    res_land = land_rhs.reshape(-1, LOW)
    damp_land = land_damp.reshape(-1, LOW)
    res_key = fold_key(key_rhs)
    damp_key = fold_key(key_damp)
    both = ("lm", "kf")

    def inner(a_land, b_land, a_key, b_key):
        return jnp.sum(a_land * b_land) + jnp.sum(a_key * b_key)

    dir_land, dir_key = res_land, res_key
    sol_land = jnp.zeros_like(res_land)
    sol_key = jnp.zeros_like(res_key)
    norm_now = lax.psum(inner(res_land, res_land, res_key, res_key), both)
    for iteration in range(ITERS):
        land_table = lax.all_gather(dir_land, "kf", axis=0, tiled=True)
        key_table = lax.all_gather(dir_key, "lm", axis=0, tiled=True)
        window = window_product(preint, dir_key)
        sum_land, sum_key = observe(
            live_blocks, land_table, key_table, land_jac, key_jac, land_pos, key_pos
        )
        prod_land = lax.psum_scatter(sum_land, "kf", scatter_dimension=0, tiled=True)
        prod_key = lax.psum_scatter(sum_key, "lm", scatter_dimension=0, tiled=True)
        prod_land = prod_land + damp_land * dir_land
        prod_key = prod_key + damp_key * dir_key + window
        step_size = norm_now / lax.psum(inner(dir_land, prod_land, dir_key, prod_key), both)
        sol_land = sol_land + step_size * dir_land
        sol_key = sol_key + step_size * dir_key
        if iteration == ITERS - 1:
            break
        res_land = res_land - step_size * prod_land
        res_key = res_key - step_size * prod_key
        norm_next = lax.psum(inner(res_land, res_land, res_key, res_key), both)
        dir_land = res_land + norm_next / norm_now * dir_land
        dir_key = res_key + norm_next / norm_now * dir_key
        norm_now = norm_next
    return sol_land.reshape(land_shape), unfold_key(sol_key)


def solution(mesh):
    split = P(None, ("lm", "kf"))
    line = P(("lm", "kf"))
    in_specs = (split,) * 6 + (line, line, line, split)
    return jax.shard_map(
        shards, mesh=mesh, in_specs=in_specs, out_specs=(split, split), check_vma=False
    )
```

time: 733 us -> 360 us (0.49)
  waiting for transfers between devices: 338 us -> 93.3 us
  matrix products: 81.8 us -> 0 us
  Pallas kernels: 0 us -> 55.5 us
  other arithmetic: 65.7 us -> 10.8 us
  local copies, waits for them, and re-layouts: 54.9 us -> 6.63 us
    unnamed x6 -> x4, waiting for transfers between devices: 189 us -> 1.25 us
    psum x2 -> x0, waiting for transfers between devices: 149 us -> none  [shards(): prod_key = lax.psum(summed_key + placed, 'lm')]
    reduce_scatter x0 -> x4, waiting for transfers between devices: none -> 92.1 us  [the longest x2 67.3 us: shards(): prod_key = lax.psum_scatter(sum_key, 'lm', scatter_dimension=0, tiled=True)]
    dot_general x48 -> x0, matrix products: 81.8 us -> none  [the longest x24 44.1 us: spread_columns(): lax.dot_general(placed, low_hot, (((1,), (1,)), ((), ())), precision=lax....]
    pallas_call x0 -> x4, Pallas kernels: none -> 55.5 us  [the longest x2 45.2 us: observe(): pl.pallas_call(observe_kernel, out_shape=(jax.ShapeDtypeStruct((land_rows...]
    dynamic_slice x26 -> x0, local copies, waits for them, and re-layouts: 22.7 us -> none  [the longest x12 11.7 us: one_turn(): lax.dynamic_slice_in_dim(key_jac, start, span, 1).reshape(2, SDIM, span)]
    select_n x36 -> x0, other arithmetic: 17.4 us -> none  [the longest x24 8.76 us: split_tables(): positions[None, :] % low_width]
    unnamed x28 -> x20, local copies, waits for them, and re-layouts: 17.3 us -> 4.13 us
  transfers between devices with their start and end apart: 4 -> 4, of which waited for: 4 -> 4; matrix products, arithmetic and copies ran while one was open for 2% -> 1% of each run, Pallas kernels for 0% -> 3%
where the time goes in v1:
time: 360 us; the launch traced here: 359 us
  blocking collectives  168 us (47%)
  waiting for transfers between devices  93.3 us (26%)
  Pallas kernels  55.5 us (15%)
  between operations  23.9 us (7%)
  other arithmetic  10.8 us (3%)
  local copies, waits for them, and re-layouts  6.63 us (2%)
    reduce_scatter x2, waiting for transfers between devices, shards(): prod_key = lax.psum_scatter(sum_key, 'lm', scatter_dimension=0, tiled=True)  67.3 us
    pallas_call x2, Pallas kernels, observe(): pl.pallas_call(observe_kernel, out_shape=(jax.ShapeDtypeStruct((land_rows...  45.2 us
    psum x1, blocking collectives, shards(): norm_next = lax.psum(inner(res_land, res_land, res_key, res_key), both)  41.2 us
    psum x1, blocking collectives, shards(): norm_now = lax.psum(inner(res_land, res_land, res_key, res_key), both)  39.4 us
    psum x1, blocking collectives, shards(): lax.psum(inner(dir_land, prod_land, dir_key, prod_key), both)  39.4 us
    all_gather x2, blocking collectives, shards(): land_table = lax.all_gather(dir_land, 'kf', axis=0, tiled=True)  27.5 us
    reduce_scatter x2, waiting for transfers between devices, shards(): lax.psum_scatter(sum_land, 'kf', scatter_dimension=0, tiled=True)  24.8 us
    all_gather x2, blocking collectives, shards(): key_table = lax.all_gather(dir_key, 'lm', axis=0, tiled=True)  21 us
  transfers between devices with their start and end apart: 4, of which 4 were waited for; matrix products, arithmetic and copies ran while one was open for 1% of the time, Pallas kernels for 3%

profile of v1, /device:TPU:0, one launch (start us, length us, event | category | flops | bytes accessed | tf_op | source)
XLA Modules:
  0.0 358.8 jit_solution(13938995663232028028)
XLA Ops:
  7.2 0.0 copy-start.6
  7.2 0.0 copy-start.5
  7.2 0.0 copy-start.3
  7.2 0.0 copy-start.8
  7.2 0.0 copy-start.7
  7.2 0.0 reduce-scatter.5.cloned.1.call-start
  7.3 0.9 reshape.31
  8.1 0.6 multiply_reduce_fusion.6
  8.8 10.8 %all_gather.13.kt_ref = f32[256,256]{1,0:T(8,128)S(1)} all-gather(f32[32,256]{1,0:T(8,128)S(1)} %bitcast.37), channel_id=1, replica_groups=mesh['lm'=8,'kf'=4] {'lm'}, dimensions={0}, use_global_device_ids=true | all-gather | bytes 294912 | tf_op jit(solution)/shard_map/all_gather | solution.py:245
  19.5 0.9 reshape.32
  20.4 13.9 %all_gather.12.lt_ref = f32[192,256]{1,0:T(8,128)S(1)} all-gather(f32[48,256]{1,0:T(8,128)S(1)} %reshape.32), channel_id=1, replica_groups=mesh['lm'=8,'kf'=4] {'kf'}, dimensions={0}, use_global_device_ids=true | all-gather | bytes 245760 | tf_op jit(solution)/shard_map/all_gather | solution.py:244
  34.3 0.9 fusion.2
  35.9 0.0 copy-start
  35.9 1.6 copy-done
  37.5 1.0 copy-done.2
  38.5 0.8 copy-done.4
  39.4 22.6 %shard_map.113 = (f32[192,256]{1,0:T(8,128)}, f32[256,256]{1,0:T(8,128)}) custom-call(s32[1]{0:T(128)S(6)} %copy.20.live_ref, f32[192,256]{1,0:T(8,128)S(1)} %all_gather.12.lt_ref, f32[256,256]{1,0:T(8,128)S(1)} %all_gather.13.kt_ref, f32[6,16384]{1,0:T(8,128)S(1)} %copy-done.2, f32[30,16384]{1,0:T(8,128)S(1)} %copy-done, s32[1,16384]{1,0:T(1,128)S(1)} %bitcast.41, ...), custom_call_target="tpu_custom_call" | custom-call | tf_op jit(solution)/shard_map/pallas_call | solution.py:114
  61.9 0.0 reduce-scatter.5.cloned.1.call-update
  62.0 0.0 reduce-scatter.7.cloned.1.call-start
  62.0 0.7 reduce-scatter.7.cloned.1.call-update
  62.7 0.0 reduce-scatter.9.cloned.1.call-start
  62.8 5.2 %shard_map.114 = f32[32,256]{1,0:T(8,128)S(1)} custom-call(f32[240,7680]{1,0:T(8,128)} %pre_ref.3, f32[32,256]{1,0:T(8,128)S(1)} %bitcast.38), custom_call_target="tpu_custom_call" | custom-call | tf_op jit(solution)/shard_map/pallas_call | solution.py:196
  67.9 0.0 copy-done.8
  68.1 0.0 copy-done.6
  68.1 0.6 multiply_reduce_fusion
  70.0 11.8 %reduce-scatter.5.cloned.1.call-done = f32[48,256]{1,0:T(8,128)} async-done(((f32[192,256]{1,0:T(8,128)}), f32[48,256]{1,0:T(8,128)}) %reduce-scatter.5.cloned.1.call-update) | async-done | bytes 49168 | tf_op jit(solution)/shard_map/reduce_scatter | solution.py:250
  81.9 1.4 multiply_reduce_fusion.3
  83.3 33.8 %reduce-scatter.7.cloned.1.call-done = f32[32,256]{1,0:T(8,128)} async-done(((f32[256,256]{1,0:T(8,128)}), f32[32,256]{1,0:T(8,128)}) %reduce-scatter.7.cloned.1.call-update) | async-done | bytes 32784 | tf_op jit(solution)/shard_map/reduce_scatter | solution.py:251
  117.0 1.4 multiply_reduce_fusion.5
  119.7 39.4 %all-reduce.2 = (f32[]{:T(128)}, f32[]{:T(128)}) all-reduce(f32[]{:T(128)S(6)} %add.73, f32[]{:T(128)S(6)} %add.79), channel_id=1, replica_groups=mesh['lm'=8,'kf'=4] {'lm','kf'}, use_global_device_ids=true, to_apply=%region_2.3 | all-reduce | flops 2 | bytes 16 | tf_op jit(solution)/shard_map/psum | solution.py:242
  160.4 0.7 multiply_reduce_fusion.4
  161.1 1.4 multiply_reduce_fusion.2
  163.9 41.2 %psum.30 = f32[]{:T(128)} all-reduce(f32[]{:T(128)S(6)} %add.80), channel_id=1, replica_groups=mesh['lm'=8,'kf'=4] {'lm','kf'}, use_global_device_ids=true, to_apply=%region_10.11 | all-reduce | flops 1 | bytes 8 | tf_op jit(solution)/shard_map/psum | solution.py:261
  206.4 10.3 %all_gather.15.kt_ref = f32[256,256]{1,0:T(8,128)S(1)} all-gather(f32[32,256]{1,0:T(8,128)S(1)} %multiply_add_fusion.4.dir_ref), channel_id=1, replica_groups=mesh['lm'=8,'kf'=4] {'lm'}, dimensions={0}, use_global_device_ids=true | all-gather | bytes 294912 | tf_op jit(solution)/shard_map/all_gather | solution.py:245
  216.7 0.8 multiply_add_fusion.1
  217.5 13.6 %all_gather.14.lt_ref = f32[192,256]{1,0:T(8,128)S(1)} all-gather(f32[48,256]{1,0:T(8,128)S(1)} %multiply_add_fusion.1), channel_id=1, replica_groups=mesh['lm'=8,'kf'=4] {'kf'}, dimensions={0}, use_global_device_ids=true | all-gather | bytes 245760 | tf_op jit(solution)/shard_map/all_gather | solution.py:244
  231.1 22.6 %shard_map.115 = (f32[192,256]{1,0:T(8,128)}, f32[256,256]{1,0:T(8,128)}) custom-call(s32[1]{0:T(128)S(6)} %copy.20.live_ref, f32[192,256]{1,0:T(8,128)S(1)} %all_gather.14.lt_ref, f32[256,256]{1,0:T(8,128)S(1)} %all_gather.15.kt_ref, f32[6,16384]{1,0:T(8,128)S(1)} %copy-done.3, f32[30,16384]{1,0:T(8,128)S(1)} %copy-done.1, s32[1,16384]{1,0:T(1,128)S(1)} %bitcast.42, ...), custom_call_target="tpu_custom_call" | custom-call | tf_op jit(solution)/shard_map/pallas_call | solution.py:114
  253.7 0.0 reduce-scatter.9.cloned.1.call-update
  253.7 0.0 reduce-scatter.11.cloned.1.call-start
  253.8 0.5 reduce-scatter.11.cloned.1.call-update
  254.3 5.2 %shard_map.116 = f32[32,256]{1,0:T(8,128)S(1)} custom-call(f32[240,7680]{1,0:T(8,128)} %pre_ref.3, f32[32,256]{1,0:T(8,128)S(1)} %multiply_add_fusion.4.dir_ref), custom_call_target="tpu_custom_call" | custom-call | tf_op jit(solution)/shard_map/pallas_call | solution.py:196
  259.5 12.9 %reduce-scatter.9.cloned.1.call-done = f32[48,256]{1,0:T(8,128)} async-done(((f32[192,256]{1,0:T(8,128)}), f32[48,256]{1,0:T(8,128)}) %reduce-scatter.9.cloned.1.call-update) | async-done | bytes 49168 | tf_op jit(solution)/shard_map/reduce_scatter | solution.py:250
  272.4 1.4 multiply_reduce_fusion.1
  273.8 33.6 %reduce-scatter.11.cloned.1.call-done = f32[32,256]{1,0:T(8,128)} async-done(((f32[256,256]{1,0:T(8,128)}), f32[32,256]{1,0:T(8,128)}) %reduce-scatter.11.cloned.1.call-update) | async-done | bytes 32784 | tf_op jit(solution)/shard_map/reduce_scatter | solution.py:251
  307.4 1.5 fusion.11
  310.2 39.4 %psum.31 = f32[]{:T(128)} all-reduce(f32[]{:T(128)S(6)} %add.86), channel_id=1, replica_groups=mesh['lm'=8,'kf'=4] {'lm','kf'}, use_global_device_ids=true, to_apply=%region_15.16 | all-reduce | flops 1 | bytes 8 | tf_op jit(solution)/shard_map/psum | solution.py:254
  351.0 0.6 copy.15
  351.6 0.7 reshape.37
  (18 shorter events, 0.2 us)
Async XLA Ops:
  7.2 60.9 %copy-start.6 = (f32[3,4096]{1,0:T(4,128)S(1)}, f32[3,4096]{1,0:T(4,128)}, u32[]{:S(2)}) copy-start(f32[3,4096]{1,0:T(4,128)} %param.10) | copy-start | bytes 147460
  7.2 223.9 %copy-start.5 = (s32[16384]{0:T(1024)S(1)}, s32[16384]{0:T(1024)}, u32[]{:S(2)}) copy-start(s32[16384]{0:T(1024)} %param.16) | copy-start | bytes 196612
  7.2 223.9 %copy-start.3 = (f32[6,16384]{1,0:T(8,128)S(1)}, f32[6,16384]{1,0:T(8,128)}, u32[]{:S(2)}) copy-start(f32[6,16384]{1,0:T(8,128)} %lj_ref.3) | copy-start | bytes 1179652
  7.2 60.7 %copy-start.8 = (f32[15,512]{1,0:T(8,128)S(1)}, f32[15,512]{1,0:T(8,128)}, u32[]{:S(2)}) copy-start(f32[15,512]{1,0:T(8,128)} %param.13) | copy-start | bytes 92164
  7.2 60.8 %copy-start.7 = (f32[3,4096]{1,0:T(4,128)S(1)}, f32[3,4096]{1,0:T(4,128)}, u32[]{:S(2)}) copy-start(f32[3,4096]{1,0:T(4,128)} %param.12) | copy-start | bytes 147460
  7.2 74.6 %reduce-scatter.5.cloned.1.call-start = ((), (), s32[]{:S(2)}) async-start(), calls=%async_computation.4 | async-start | bytes 245760 | tf_op jit(solution)/shard_map/reduce_scatter | solution.py:250
  35.9 1.6 copy-start
  37.5 1.0 copy-start.2
  38.5 0.8 copy-start.4
  39.3 191.8 %copy-start.1 = (f32[30,16384]{1,0:T(8,128)S(1)}, f32[30,16384]{1,0:T(8,128)}, u32[]{:S(2)}) copy-start(f32[30,16384]{1,0:T(8,128)} %kj_ref.3) | copy-start | bytes 5898244
  62.0 55.1 %reduce-scatter.7.cloned.1.call-start = ((), (), s32[]{:S(2)}) async-start(), calls=%async_computation.5 | async-start | bytes 294912 | tf_op jit(solution)/shard_map/reduce_scatter | solution.py:251
  62.7 209.7 %reduce-scatter.9.cloned.1.call-start = ((), (), s32[]{:S(2)}) async-start(), calls=%async_computation.6 | async-start | bytes 245760 | tf_op jit(solution)/shard_map/reduce_scatter | solution.py:250
  253.7 53.7 %reduce-scatter.11.cloned.1.call-start = ((), (), s32[]{:S(2)}) async-start(), calls=%async_computation.7 | async-start | bytes 294912 | tf_op jit(solution)/shard_map/reduce_scatter | solution.py:251
Sparse Core Ops, SparseCore 0:
  62.1 19.7 reduce-scatter.4
  85.2 31.8 reduce-scatter.6
  253.9 18.5 reduce-scatter.8
  275.6 31.7 reduce-scatter.10

commit v2 on v1

--- a/solution.py
+++ b/solution.py
@@ -1,4 +1,3 @@
-import functools
 import jax
 import jax.numpy as jnp
 from jax import lax
@@ -9,7 +8,6 @@
 WSTATES = 16
 SDIM = 15
 BLOCK = 128
-ITERS = 2
 WPAR = 240
 LOW = 256
 CHUNK = 1024
@@ -217,51 +215,246 @@
     return parts.reshape(SDIM, -1)
 
 
+def greet():
+    barrier = pltpu.get_barrier_semaphore()
+    count = 0
+    for axis in ("lm", "kf"):
+        size = lax.axis_size(axis)
+        place = lax.axis_index(axis)
+        for hop in range(1, size):
+            pl.semaphore_signal(
+                barrier,
+                inc=1,
+                device_id={axis: lax.rem(place + hop, size)},
+                device_id_type=pl.DeviceIdType.MESH,
+            )
+            count += 1
+    pl.semaphore_wait(barrier, count)
+
+
+def send(axis, source, target, sems):
+    size = lax.axis_size(axis)
+    place = lax.axis_index(axis)
+    copies = []
+    for hop in range(1, size):
+        peer = lax.rem(place + hop, size)
+        copy = pltpu.make_async_remote_copy(
+            src_ref=source(peer, hop),
+            dst_ref=target(peer, hop),
+            send_sem=sems.at[0, hop - 1],
+            recv_sem=sems.at[1, hop - 1],
+            device_id={axis: peer},
+            device_id_type=pl.DeviceIdType.MESH,
+        )
+        copy.start()
+        copies.append(copy)
+    return copies
+
+
+def finish(copies):
+    for copy in copies:
+        copy.wait()
+
+
+def gather_start(axis, table, sems):
+    place = lax.axis_index(axis)
+    mine = table.at[place]
+    return send(axis, lambda peer, hop: mine, lambda peer, hop: mine, sems)
+
+
+def scatter_start(axis, parts, slots, sems):
+    return send(
+        axis, lambda peer, hop: parts.at[peer], lambda peer, hop: slots.at[hop - 1], sems
+    )
+
+
+def scatter_total(axis, parts, slots):
+    total = parts[lax.axis_index(axis)]
+    for hop in range(1, lax.axis_size(axis)):
+        total = total + slots[hop - 1]
+    return total
+
+
+def sum_all(tile, kf_slots, lm_slots, kf_sems, lm_sems):
+    for axis, slots, sems in (("kf", kf_slots, kf_sems), ("lm", lm_slots, lm_sems)):
+        slots[lax.axis_index(axis)] = tile
+        finish(gather_start(axis, slots, sems))
+        tile = slots[0]
+        for place in range(1, lax.axis_size(axis)):
+            tile = tile + slots[place]
+    return tile
+
+
+def inner(a_land, b_land, a_key, b_key):
+    return jnp.sum(a_land * b_land, keepdims=True) + jnp.sum(a_key * b_key, keepdims=True)
+
+
+def two_rows(first, second):
+    rows = lax.broadcasted_iota(jnp.int32, (8, 128), 0)
+    return jnp.where(rows == 0, first, second)
+
+
+def gather_kernel(land_ref, key_ref, lt_ref, kt_ref, lsems, ksems):
+    greet()
+    lt_ref[lax.axis_index("kf")] = land_ref[...]
+    kt_ref[lax.axis_index("lm")] = key_ref[...]
+    copies = gather_start("kf", lt_ref, lsems) + gather_start("lm", kt_ref, ksems)
+    finish(copies)
+
+
+def step_kernel(
+    sl_ref, sk_ref, lt_ref, kt_ref, ld_ref, kd_ref, win_ref,
+    rl_ref, rk_ref, own_ref, ql_ref, qk_ref, scal_ref,
+    lslots, kslots, kf_slots, lm_slots, lsems, ksems, lgs, kgs, kfs, lms,
+):
+    greet()
+    kf_place = lax.axis_index("kf")
+    lm_place = lax.axis_index("lm")
+    copies = scatter_start("kf", sl_ref, lslots, lsems)
+    copies += scatter_start("lm", sk_ref, kslots, ksems)
+    dir_land = lt_ref[kf_place]
+    dir_key = kt_ref[lm_place]
+    norm = inner(dir_land, dir_land, dir_key, dir_key)
+    finish(copies)
+    prod_land = scatter_total("kf", sl_ref, lslots) + ld_ref[...] * dir_land
+    prod_key = scatter_total("lm", sk_ref, kslots) + kd_ref[...] * dir_key + win_ref[...]
+    rl_ref[kf_place] = prod_land
+    rk_ref[lm_place] = prod_key
+    copies = gather_start("kf", rl_ref, lgs) + gather_start("lm", rk_ref, kgs)
+    ql_ref[...] = prod_land
+    qk_ref[...] = prod_key
+    tile = two_rows(norm, inner(dir_land, prod_land, dir_key, prod_key))
+    tile = sum_all(tile, kf_slots, lm_slots, kfs, lms)
+    norm = tile[0:1, 0:1]
+    step = norm / tile[1:2, 0:1]
+    scal_ref[...] = two_rows(norm, step)
+    own_ref[...] = dir_key - step * prod_key
+    finish(copies)
+    rl_ref[...] = lt_ref[...] - step[None] * rl_ref[...]
+    rk_ref[...] = kt_ref[...] - step[None] * rk_ref[...]
+
+
+def last_kernel(
+    sl_ref, sk_ref, dl_ref, dk_ref, ql_ref, qk_ref, ld_ref, kd_ref, win_ref, scal_ref,
+    ol_ref, ok_ref,
+    lslots, kslots, kf_slots, lm_slots, kf_more, lm_more, lsems, ksems, kfs, lms, kft, lmt,
+):
+    greet()
+    copies = scatter_start("kf", sl_ref, lslots, lsems)
+    copies += scatter_start("lm", sk_ref, kslots, ksems)
+    norm = scal_ref[0:1, 0:1]
+    step = scal_ref[1:2, 0:1]
+    old_land, old_key = dl_ref[...], dk_ref[...]
+    prod_land, prod_key = ql_ref[...], qk_ref[...]
+    res_land = old_land - step * prod_land
+    res_key = old_key - step * prod_key
+    part = inner(res_land, res_land, res_key, res_key)
+    tile = sum_all(two_rows(part, part), kf_slots, lm_slots, kfs, lms)
+    norm_next = tile[0:1, 0:1]
+    beta = norm_next / norm
+    dir_land = res_land + beta * old_land
+    dir_key = res_key + beta * old_key
+    finish(copies)
+    new_land = scatter_total("kf", sl_ref, lslots) + ld_ref[...] * res_land
+    new_key = scatter_total("lm", sk_ref, kslots) + kd_ref[...] * res_key + win_ref[...]
+    new_land = new_land + beta * prod_land
+    new_key = new_key + beta * prod_key
+    part = inner(dir_land, new_land, dir_key, new_key)
+    tile = sum_all(two_rows(part, part), kf_more, lm_more, kft, lmt)
+    next_step = norm_next / tile[0:1, 0:1]
+    ol_ref[...] = step * old_land + next_step * dir_land
+    ok_ref[...] = step * old_key + next_step * dir_key
+
+
+def exchange(kernel, identity, outs, scratch, *operands):
+    vmem = pl.BlockSpec(memory_space=pltpu.VMEM)
+    return pl.pallas_call(
+        kernel,
+        out_shape=tuple(jax.ShapeDtypeStruct(shape, F32) for shape in outs),
+        in_specs=[vmem] * len(operands),
+        out_specs=(vmem,) * len(outs),
+        scratch_shapes=scratch,
+        compiler_params=pltpu.CompilerParams(
+            collective_id=identity, has_side_effects=True, vmem_limit_bytes=16 * 2**20
+        ),
+    )(*operands)
+
+
 def shards(
     land_rhs, key_rhs, land_damp, key_damp, land_jac, key_jac,
     obs_landmark, obs_keyframe, live_blocks, preint,
 ):
     state_dev = key_rhs.shape[1]
     kf_count = lax.axis_size("kf")
+    lm_count = lax.axis_size("lm")
     key_pos = obs_keyframe // state_dev // kf_count * state_dev + obs_keyframe % state_dev
     key_pos = key_pos[None]
     land_pos = obs_landmark[None]
     land_shape = land_rhs.shape
-    res_land = land_rhs.reshape(-1, LOW)
+    dir_land = land_rhs.reshape(-1, LOW)
     damp_land = land_damp.reshape(-1, LOW)
-    res_key = fold_key(key_rhs)
+    dir_key = fold_key(key_rhs)
     damp_key = fold_key(key_damp)
-    both = ("lm", "kf")
-
-    def inner(a_land, b_land, a_key, b_key):
-        return jnp.sum(a_land * b_land) + jnp.sum(a_key * b_key)
-
-    dir_land, dir_key = res_land, res_key
-    sol_land = jnp.zeros_like(res_land)
-    sol_key = jnp.zeros_like(res_key)
-    norm_now = lax.psum(inner(res_land, res_land, res_key, res_key), both)
-    for iteration in range(ITERS):
-        land_table = lax.all_gather(dir_land, "kf", axis=0, tiled=True)
-        key_table = lax.all_gather(dir_key, "lm", axis=0, tiled=True)
-        window = window_product(preint, dir_key)
-        sum_land, sum_key = observe(
-            live_blocks, land_table, key_table, land_jac, key_jac, land_pos, key_pos
+    own_land, own_key = dir_land.shape, dir_key.shape
+    all_land, all_key = (kf_count,) + own_land, (lm_count,) + own_key
+
+    kf_sems = pltpu.SemaphoreType.DMA((2, kf_count - 1))
+    lm_sems = pltpu.SemaphoreType.DMA((2, lm_count - 1))
+    slots = [
+        pltpu.VMEM((kf_count - 1,) + own_land, F32),
+        pltpu.VMEM((lm_count - 1,) + own_key, F32),
+    ]
+    tiles = [pltpu.VMEM((kf_count, 8, 128), F32), pltpu.VMEM((lm_count, 8, 128), F32)]
+    sems = [kf_sems, lm_sems]
+
+    def seen(land_table, key_table):
+        land, key = observe(
+            live_blocks,
+            land_table.reshape(-1, LOW),
+            key_table.reshape(-1, LOW),
+            land_jac,
+            key_jac,
+            land_pos,
+            key_pos,
         )
-        prod_land = lax.psum_scatter(sum_land, "kf", scatter_dimension=0, tiled=True)
-        prod_key = lax.psum_scatter(sum_key, "lm", scatter_dimension=0, tiled=True)
-        prod_land = prod_land + damp_land * dir_land
-        prod_key = prod_key + damp_key * dir_key + window
-        step_size = norm_now / lax.psum(inner(dir_land, prod_land, dir_key, prod_key), both)
-        sol_land = sol_land + step_size * dir_land
-        sol_key = sol_key + step_size * dir_key
-        if iteration == ITERS - 1:
-            break
-        res_land = res_land - step_size * prod_land
-        res_key = res_key - step_size * prod_key
-        norm_next = lax.psum(inner(res_land, res_land, res_key, res_key), both)
-        dir_land = res_land + norm_next / norm_now * dir_land
-        dir_key = res_key + norm_next / norm_now * dir_key
-        norm_now = norm_next
+        return land.reshape(all_land), key.reshape(all_key)
+
+    land_table, key_table = exchange(
+        gather_kernel, 1, (all_land, all_key), sems, dir_land, dir_key
+    )
+    window = window_product(preint, dir_key)
+    sum_land, sum_key = seen(land_table, key_table)
+    res_land, res_key, own_res, prod_land, prod_key, scal = exchange(
+        step_kernel,
+        2,
+        (all_land, all_key, own_key, own_land, own_key, (8, 128)),
+        slots + tiles + sems * 3,
+        sum_land,
+        sum_key,
+        land_table,
+        key_table,
+        damp_land,
+        damp_key,
+        window,
+    )
+    window = window_product(preint, own_res)
+    sum_land, sum_key = seen(res_land, res_key)
+    sol_land, sol_key = exchange(
+        last_kernel,
+        3,
+        (own_land, own_key),
+        slots + tiles * 2 + sems * 3,
+        sum_land,
+        sum_key,
+        dir_land,
+        dir_key,
+        prod_land,
+        prod_key,
+        damp_land,
+        damp_key,
+        window,
+        scal,
+    )
     return sol_land.reshape(land_shape), unfold_key(sol_key)
 
 

time: 360 us -> 107 us (0.30)
  blocking collectives: 168 us -> 0 us
  waiting for transfers between devices: 93.3 us -> 0 us
  Pallas kernels: 55.5 us -> 102 us
  between operations: 23.9 us -> 1.66 us
  other arithmetic: 10.8 us -> 0.1 us
    psum x3 -> x0, blocking collectives: 120 us -> none  [the longest x1 41.2 us: shards(): norm_next = lax.psum(inner(res_land, res_land, res_key, res_key), both)]
    reduce_scatter x4 -> x0, waiting for transfers between devices: 92.1 us -> none  [the longest x2 67.3 us: shards(): prod_key = lax.psum_scatter(sum_key, 'lm', scatter_dimension=0, tiled=True)]
    all_gather x4 -> x0, blocking collectives: 48.5 us -> none  [the longest x2 27.5 us: shards(): land_table = lax.all_gather(dir_land, 'kf', axis=0, tiled=True)]
    pallas_call x0 -> x3, Pallas kernels: none -> 47.8 us  [exchange(): pl.pallas_call(kernel, out_shape=tuple((jax.ShapeDtypeStruct(shape, F32)...]
    reduce_sum x8 -> x0, other arithmetic: 9.02 us -> none  [inner(): return jnp.sum(a_land * b_land) + jnp.sum(a_key * b_key)]
  transfers between devices with their start and end apart: 4 -> 0, of which waited for: 4 -> 0; matrix products, arithmetic and copies ran while one was open for 1% -> 0% of each run, Pallas kernels for 3% -> 0%
where the time goes in v2:
time: 107 us
  Pallas kernels  102 us (95%)
  local copies, waits for them, and re-layouts  3.07 us (3%)
  between operations  1.66 us (2%)
    pallas_call x3, Pallas kernels, exchange(): pl.pallas_call(kernel, out_shape=tuple((jax.ShapeDtypeStruct(shape, F32)...  47.8 us
    pallas_call x2, Pallas kernels, observe(): pl.pallas_call(observe_kernel, out_shape=(jax.ShapeDtypeStruct((land_rows...  43.7 us
    pallas_call x2, Pallas kernels, window_product(): pl.pallas_call(window_kernel, out_shape=jax.ShapeDtypeStruct(direction.sh...  10.3 us

profile of v2, /device:TPU:0, one launch (start us, length us, event | category | flops | bytes accessed | tf_op | source)
XLA Modules:
  0.0 106.7 jit_solution(12378281285628151841)
XLA Ops:
  0.6 0.0 copy-start
  0.6 0.0 copy-start.1
  0.7 0.0 copy-start.5
  0.7 0.0 copy-start.2
  0.7 0.0 copy-start.4
  0.7 0.0 copy-start.3
  1.5 0.8 reshape.56
  2.4 0.8 reshape.63
  3.2 5.2 %shard_map.115.win_ref = f32[32,256]{1,0:T(8,128)S(1)} custom-call(f32[240,7680]{1,0:T(8,128)} %pre_ref.3, f32[32,256]{1,0:T(8,128)S(1)} %bitcast.28), custom_call_target="tpu_custom_call" | custom-call | tf_op jit(solution)/shard_map/pallas_call | solution.py:194
  8.3 0.0 copy-done.3
  8.4 0.0 copy-done.4
  8.5 0.0 copy-done.5
  8.5 0.1 fusion.2
  8.6 11.4 %shard_map.113 = (f32[4,48,256]{2,1,0:T(8,128)S(1)}, f32[8,32,256]{2,1,0:T(8,128)S(1)}) custom-call(f32[48,256]{1,0:T(8,128)S(1)} %reshape.55.land_ref.dl_ref, f32[32,256]{1,0:T(8,128)S(1)} %bitcast.29), custom_call_target="tpu_custom_call" | custom-call | tf_op jit(solution)/shard_map/pallas_call | solution.py:371
  19.9 0.0 copy-done
  20.0 0.0 copy-done.1
  20.0 0.0 copy-done.2
  20.0 21.9 %shard_map.114 = (f32[192,256]{1,0:T(8,128)S(1)}, f32[256,256]{1,0:T(8,128)S(1)}) custom-call(s32[1]{0:T(128)S(6)} %copy.20.live_ref, f32[192,256]{1,0:T(8,128)S(1)} %bitcast.25, f32[256,256]{1,0:T(8,128)S(1)} %bitcast.24, f32[6,16384]{1,0:T(8,128)S(1)} %copy-done.1, f32[30,16384]{1,0:T(8,128)S(1)} %copy-done, s32[1,16384]{1,0:T(1,128)S(1)} %bitcast.34, ...), custom_call_target="tpu_custom_call" | custom-call | tf_op jit(solution)/shard_map/pallas_call | solution.py:112
  41.8 17.5 %shard_map.116 = (f32[4,48,256]{2,1,0:T(8,128)S(1)}, f32[8,32,256]{2,1,0:T(8,128)S(1)}, f32[32,256]{1,0:T(8,128)S(1)}, f32[48,256]{1,0:T(8,128)S(1)}, f32[32,256]{1,0:T(8,128)S(1)}, /*index=5*/f32[8,128]{1,0:T(8,128)S(1)}) custom-call(f32[4,48,256]{2,1,0:T(8,128)S(1)} %bitcast.39, f32[8,32,256]{2,1,0:T(8,128)S(1)} %bitcast.36, ...), custom_call_target="tpu_custom_call" | custom-call | tf_op jit(solution)/shard_map/pallas_call | solution.py:371
  59.4 21.9 %shard_map.117 = (f32[192,256]{1,0:T(8,128)S(1)}, f32[256,256]{1,0:T(8,128)S(1)}) custom-call(s32[1]{0:T(128)S(6)} %copy.20.live_ref, f32[192,256]{1,0:T(8,128)S(1)} %bitcast.40, f32[256,256]{1,0:T(8,128)S(1)} %bitcast.37, f32[6,16384]{1,0:T(8,128)S(1)} %copy-done.1, f32[30,16384]{1,0:T(8,128)S(1)} %copy-done, s32[1,16384]{1,0:T(1,128)S(1)} %bitcast.35, ...), custom_call_target="tpu_custom_call" | custom-call | tf_op jit(solution)/shard_map/pallas_call | solution.py:112
  81.2 5.2 %shard_map.118.win_ref = f32[32,256]{1,0:T(8,128)S(1)} custom-call(f32[240,7680]{1,0:T(8,128)} %pre_ref.3, f32[32,256]{1,0:T(8,128)S(1)} %get-tuple-element.26.dir_ref), custom_call_target="tpu_custom_call" | custom-call | tf_op jit(solution)/shard_map/pallas_call | solution.py:194
  86.4 18.9 %shard_map.119 = (f32[48,256]{1,0:T(8,128)S(1)}, f32[32,256]{1,0:T(8,128)S(1)}) custom-call(f32[4,48,256]{2,1,0:T(8,128)S(1)} %bitcast.38, f32[8,32,256]{2,1,0:T(8,128)S(1)} %bitcast.33, f32[48,256]{1,0:T(8,128)S(1)} %reshape.55.land_ref.dl_ref, f32[32,256]{1,0:T(8,128)S(1)} %bitcast.30, f32[48,256]{1,0:T(8,128)S(1)} %get-tuple-element.24.ql_ref, ...), custom_call_target="tpu_custom_call" | custom-call | tf_op jit(solution)/shard_map/pallas_call | solution.py:371
  105.4 0.6 copy.15
  106.0 0.7 reshape.69
  (9 shorter events, 0.1 us)
Async XLA Ops:
  0.6 19.3 %copy-start = (f32[30,16384]{1,0:T(8,128)S(1)}, f32[30,16384]{1,0:T(8,128)}, u32[]{:S(2)}) copy-start(f32[30,16384]{1,0:T(8,128)} %kj_ref.3) | copy-start | bytes 5898244
  0.6 19.3 %copy-start.1 = (f32[6,16384]{1,0:T(8,128)S(1)}, f32[6,16384]{1,0:T(8,128)}, u32[]{:S(2)}) copy-start(f32[6,16384]{1,0:T(8,128)} %lj_ref.3) | copy-start | bytes 1179652
  0.7 7.8 %copy-start.5 = (s32[16384]{0:T(1024)S(1)}, s32[16384]{0:T(1024)}, u32[]{:S(2)}) copy-start(s32[16384]{0:T(1024)} %param.17) | copy-start | bytes 196612
  0.7 19.3 %copy-start.2 = (s32[16384]{0:T(1024)S(1)}, s32[16384]{0:T(1024)}, u32[]{:S(2)}) copy-start(s32[16384]{0:T(1024)} %param.16) | copy-start | bytes 196612
  0.7 7.7 %copy-start.4 = (f32[3,4096]{1,0:T(4,128)S(1)}, f32[3,4096]{1,0:T(4,128)}, u32[]{:S(2)}) copy-start(f32[3,4096]{1,0:T(4,128)} %param.12) | copy-start | bytes 147460
  0.7 7.7 %copy-start.3 = (f32[3,4096]{1,0:T(4,128)S(1)}, f32[3,4096]{1,0:T(4,128)}, u32[]{:S(2)}) copy-start(f32[3,4096]{1,0:T(4,128)} %param.10) | copy-start | bytes 147460

commit v3 on v2

--- a/solution.py
+++ b/solution.py
@@ -1,3 +1,4 @@
+import functools
 import jax
 import jax.numpy as jnp
 from jax import lax
@@ -10,7 +11,7 @@
 BLOCK = 128
 WPAR = 240
 LOW = 256
-CHUNK = 1024
+CHUNK = 4096
 F32 = jnp.float32
 BF16 = jnp.bfloat16
 
@@ -25,10 +26,12 @@
     return jnp.concatenate([high.astype(BF16), low.astype(BF16)], axis=0)
 
 
-def observe_kernel(
-    live_ref, lt_ref, kt_ref, lj_ref, kj_ref, il_ref, ik_ref, ol_ref, ok_ref,
-    lhl_ref, khl_ref, kjp_ref, lacc_ref, kacc_ref, lplace_ref, kplace_ref,
-):
+def observe_kernel(spread, live_ref, lt_ref, kt_ref, lj_ref, kj_ref, il_ref, ik_ref, *rest):
+    if spread:
+        ol_ref, ok_ref, os_ref = rest[:3]
+        lhl_ref, khl_ref, kjp_ref, lacc_ref, kacc_ref, lplace_ref, kplace_ref = rest[3:]
+    else:
+        os_ref, lhl_ref, khl_ref, kjp_ref = rest
     land_rows = lt_ref.shape[0]
     key_rows = kt_ref.shape[0]
     groups = land_rows // 48
@@ -38,8 +41,9 @@
     limit = live_ref[0] * BLOCK
     lhl_ref[...] = stacked_halves(lt_ref[...])
     khl_ref[...] = stacked_halves(kt_ref[...])
-    lacc_ref[...] = jnp.zeros_like(lacc_ref)
-    kacc_ref[...] = jnp.zeros_like(kacc_ref)
+    if spread:
+        lacc_ref[...] = jnp.zeros_like(lacc_ref)
+        kacc_ref[...] = jnp.zeros_like(kacc_ref)
     kjp_ref[...] = jnp.zeros_like(kjp_ref)
 
     def turn(index, carry):
@@ -52,10 +56,20 @@
         lhigh = lpos // LOW
         khigh = kpos // LOW
         low_iota = lax.broadcasted_iota(jnp.int32, (LOW, span), 0)
-        lhot = jnp.where(low_iota == lpos % LOW, 1.0, 0.0).astype(BF16)
-        khot = jnp.where(low_iota == kpos % LOW, 1.0, 0.0).astype(BF16)
-        lall = jnp.dot(lhl_ref[...], lhot, preferred_element_type=F32)
-        kall = jnp.dot(khl_ref[...], khot, preferred_element_type=F32)
+        low16 = low_iota.astype(F32).astype(BF16)
+        one, zero = jnp.ones((), BF16), jnp.zeros((), BF16)
+        llow = jnp.broadcast_to((lpos % LOW).astype(F32).astype(BF16), (LOW, span))
+        klow = jnp.broadcast_to((kpos % LOW).astype(F32).astype(BF16), (LOW, span))
+        lhot = jnp.where(low16 == llow, one, zero)
+        khot = jnp.where(low16 == klow, one, zero)
+        lcat = jnp.concatenate([lhl_ref[0:land_rows, :], lhl_ref[land_rows:, :]], axis=1)
+        kcat = jnp.concatenate([khl_ref[0:key_rows, :], khl_ref[key_rows:, :]], axis=1)
+        lall = jnp.dot(
+            lcat, jnp.concatenate([lhot, lhot], axis=0), preferred_element_type=F32
+        )
+        kall = jnp.dot(
+            kcat, jnp.concatenate([khot, khot], axis=0), preferred_element_type=F32
+        )
         high_iota = lax.broadcasted_iota(jnp.int32, (16, span), 0)
         lmask = [lhigh - 16 * d == high_iota for d in range(groups)]
         kmask = [jnp.broadcast_to(khigh, (16, span)) == h for h in range(highs)]
@@ -64,12 +78,12 @@
             part = jnp.zeros((16, span), F32)
             for d in range(groups):
                 row = d * 48 + c * 16
-                both = lall[row : row + 16] + lall[land_rows + row : land_rows + row + 16]
+                both = lall[row : row + 16]
                 part = jnp.where(lmask[d], both, part)
             seen_land.append(jnp.sum(part, axis=0, keepdims=True))
         seen_key = jnp.zeros((16, span), F32)
         for h in range(highs):
-            both = kall[h * 16 : h * 16 + 16] + kall[key_rows + h * 16 : key_rows + h * 16 + 16]
+            both = kall[h * 16 : h * 16 + 16]
             seen_key = jnp.where(kmask[h], both, seen_key)
         inside = start + lax.broadcasted_iota(jnp.int32, (1, span), 1) < limit
         image = []
@@ -78,20 +92,28 @@
             for c in range(3):
                 value = value + lj_ref[r * 3 + c : r * 3 + c + 1, cols] * seen_land[c]
             image.append(jnp.where(inside, value, 0.0))
+        carry = carry + image[0] * image[0] + image[1] * image[1]
+        if not spread:
+            return carry
+        lplace = (lhigh - high_iota).astype(F32).astype(BF16)
+        kplace = jnp.broadcast_to(khigh, (16, span)).astype(F32).astype(BF16)
         for c in range(3):
             back = (
                 lj_ref[c : c + 1, cols] * image[0] + lj_ref[3 + c : 4 + c, cols] * image[1]
             )
             for p, part in enumerate(halves(back)):
-                part = jnp.broadcast_to(part, (16, span))
+                part = jnp.broadcast_to(part, (16, span)).astype(BF16)
                 for d in range(groups):
                     row = p * land_rows + d * 48 + c * 16
-                    lplace_ref[row : row + 16, :] = jnp.where(lmask[d], part, 0.0).astype(BF16)
+                    here = lplace == jnp.full((), 16 * d, BF16)
+                    lplace_ref[row : row + 16, :] = jnp.where(here, part, zero)
         back = kjp_ref[0:16, :] * image[0] + kjp_ref[16:32, :] * image[1]
         for p, part in enumerate(halves(back)):
+            part = part.astype(BF16)
             for h in range(highs):
                 row = p * key_rows + h * 16
-                kplace_ref[row : row + 16, :] = jnp.where(kmask[h], part, 0.0).astype(BF16)
+                here = kplace == jnp.full((), h, BF16)
+                kplace_ref[row : row + 16, :] = jnp.where(here, part, zero)
         contract = (((1,), (1,)), ((), ()))
         lacc_ref[...] += lax.dot_general(
             lplace_ref[...], lhot, contract, preferred_element_type=F32
@@ -101,31 +123,39 @@
         )
         return carry
 
-    lax.fori_loop(0, total // span, turn, 0)
-    ol_ref[...] = lacc_ref[0:land_rows, :] + lacc_ref[land_rows:, :]
-    ok_ref[...] = kacc_ref[0:key_rows, :] + kacc_ref[key_rows:, :]
-
-
-def observe(live, land_table, key_table, land_jac, key_jac, land_pos, key_pos):
+    squares = lax.fori_loop(0, total // span, turn, jnp.zeros((1, span), F32))
+    os_ref[...] = jnp.broadcast_to(jnp.sum(squares, keepdims=True), os_ref.shape)
+    if spread:
+        ol_ref[...] = lacc_ref[0:land_rows, :] + lacc_ref[land_rows:, :]
+        ok_ref[...] = kacc_ref[0:key_rows, :] + kacc_ref[key_rows:, :]
+
+
+def observe(spread, live, land_table, key_table, land_jac, key_jac, land_pos, key_pos):
     land_rows, key_rows = land_table.shape[0], key_table.shape[0]
     vmem = pl.BlockSpec(memory_space=pltpu.VMEM)
-    return pl.pallas_call(
-        observe_kernel,
-        out_shape=(
+    outs = [jax.ShapeDtypeStruct((8, 128), F32)]
+    scratch = [
+        pltpu.VMEM((2 * land_rows, LOW), BF16),
+        pltpu.VMEM((2 * key_rows, LOW), BF16),
+        pltpu.VMEM((32, CHUNK), F32),
+    ]
+    if spread:
+        outs = [
             jax.ShapeDtypeStruct((land_rows, LOW), F32),
             jax.ShapeDtypeStruct((key_rows, LOW), F32),
-        ),
-        in_specs=[pl.BlockSpec(memory_space=pltpu.SMEM)] + [vmem] * 6,
-        out_specs=(vmem, vmem),
-        scratch_shapes=[
-            pltpu.VMEM((2 * land_rows, LOW), BF16),
-            pltpu.VMEM((2 * key_rows, LOW), BF16),
-            pltpu.VMEM((32, CHUNK), F32),
+        ] + outs
+        scratch += [
             pltpu.VMEM((2 * land_rows, LOW), F32),
             pltpu.VMEM((2 * key_rows, LOW), F32),
             pltpu.VMEM((2 * land_rows, CHUNK), BF16),
             pltpu.VMEM((2 * key_rows, CHUNK), BF16),
-        ],
+        ]
+    return pl.pallas_call(
+        functools.partial(observe_kernel, spread),
+        out_shape=tuple(outs),
+        in_specs=[pl.BlockSpec(memory_space=pltpu.SMEM)] + [vmem] * 6,
+        out_specs=(vmem,) * len(outs),
+        scratch_shapes=scratch,
         compiler_params=pltpu.CompilerParams(vmem_limit_bytes=50 * 2**20),
     )(live, land_table, key_table, land_jac, key_jac, land_pos, key_pos)
 
@@ -289,9 +319,9 @@
     return jnp.sum(a_land * b_land, keepdims=True) + jnp.sum(a_key * b_key, keepdims=True)
 
 
-def two_rows(first, second):
+def three_rows(first, second, third):
     rows = lax.broadcasted_iota(jnp.int32, (8, 128), 0)
-    return jnp.where(rows == 0, first, second)
+    return jnp.where(rows == 0, first, jnp.where(rows == 1, second, third))
 
 
 def gather_kernel(land_ref, key_ref, lt_ref, kt_ref, lsems, ksems):
@@ -303,7 +333,7 @@
 
 
 def step_kernel(
-    sl_ref, sk_ref, lt_ref, kt_ref, ld_ref, kd_ref, win_ref,
+    sl_ref, sk_ref, sq_ref, dl_ref, dk_ref, ld_ref, kd_ref, win_ref,
     rl_ref, rk_ref, own_ref, ql_ref, qk_ref, scal_ref,
     lslots, kslots, kf_slots, lm_slots, lsems, ksems, lgs, kgs, kfs, lms,
 ):
@@ -312,58 +342,54 @@
     lm_place = lax.axis_index("lm")
     copies = scatter_start("kf", sl_ref, lslots, lsems)
     copies += scatter_start("lm", sk_ref, kslots, ksems)
-    dir_land = lt_ref[kf_place]
-    dir_key = kt_ref[lm_place]
+    dir_land, dir_key = dl_ref[...], dk_ref[...]
+    damped_land = ld_ref[...] * dir_land
+    damped_key = kd_ref[...] * dir_key + win_ref[...]
     norm = inner(dir_land, dir_land, dir_key, dir_key)
+    energy = sq_ref[0:1, 0:1] + inner(dir_land, damped_land, dir_key, damped_key)
+    tile = three_rows(norm, energy, energy)
+    tile = sum_all(tile, kf_slots, lm_slots, kfs, lms)
+    norm, energy = tile[0:1, 0:1], tile[1:2, 0:1]
+    step = norm / energy
+    scal_ref[...] = three_rows(norm, energy, step)
     finish(copies)
-    prod_land = scatter_total("kf", sl_ref, lslots) + ld_ref[...] * dir_land
-    prod_key = scatter_total("lm", sk_ref, kslots) + kd_ref[...] * dir_key + win_ref[...]
-    rl_ref[kf_place] = prod_land
-    rk_ref[lm_place] = prod_key
+    prod_land = scatter_total("kf", sl_ref, lslots) + damped_land
+    prod_key = scatter_total("lm", sk_ref, kslots) + damped_key
+    res_key = dir_key - step * prod_key
+    rl_ref[kf_place] = dir_land - step * prod_land
+    rk_ref[lm_place] = res_key
     copies = gather_start("kf", rl_ref, lgs) + gather_start("lm", rk_ref, kgs)
     ql_ref[...] = prod_land
     qk_ref[...] = prod_key
-    tile = two_rows(norm, inner(dir_land, prod_land, dir_key, prod_key))
-    tile = sum_all(tile, kf_slots, lm_slots, kfs, lms)
-    norm = tile[0:1, 0:1]
-    step = norm / tile[1:2, 0:1]
-    scal_ref[...] = two_rows(norm, step)
-    own_ref[...] = dir_key - step * prod_key
+    own_ref[...] = res_key
     finish(copies)
-    rl_ref[...] = lt_ref[...] - step[None] * rl_ref[...]
-    rk_ref[...] = kt_ref[...] - step[None] * rk_ref[...]
 
 
 def last_kernel(
-    sl_ref, sk_ref, dl_ref, dk_ref, ql_ref, qk_ref, ld_ref, kd_ref, win_ref, scal_ref,
-    ol_ref, ok_ref,
-    lslots, kslots, kf_slots, lm_slots, kf_more, lm_more, lsems, ksems, kfs, lms, kft, lmt,
+    sq_ref, dl_ref, dk_ref, ql_ref, qk_ref, ld_ref, kd_ref, win_ref, scal_ref,
+    ol_ref, ok_ref, kf_slots, lm_slots, kfs, lms,
 ):
     greet()
-    copies = scatter_start("kf", sl_ref, lslots, lsems)
-    copies += scatter_start("lm", sk_ref, kslots, ksems)
     norm = scal_ref[0:1, 0:1]
-    step = scal_ref[1:2, 0:1]
+    energy = scal_ref[1:2, 0:1]
+    step = scal_ref[2:3, 0:1]
     old_land, old_key = dl_ref[...], dk_ref[...]
     prod_land, prod_key = ql_ref[...], qk_ref[...]
     res_land = old_land - step * prod_land
     res_key = old_key - step * prod_key
-    part = inner(res_land, res_land, res_key, res_key)
-    tile = sum_all(two_rows(part, part), kf_slots, lm_slots, kfs, lms)
+    own_norm = inner(res_land, res_land, res_key, res_key)
+    own_energy = sq_ref[0:1, 0:1] + inner(
+        res_land, ld_ref[...] * res_land, res_key, kd_ref[...] * res_key + win_ref[...]
+    )
+    own_cross = inner(res_land, prod_land, res_key, prod_key)
+    tile = three_rows(own_norm, own_energy, own_cross)
+    tile = sum_all(tile, kf_slots, lm_slots, kfs, lms)
     norm_next = tile[0:1, 0:1]
     beta = norm_next / norm
-    dir_land = res_land + beta * old_land
-    dir_key = res_key + beta * old_key
-    finish(copies)
-    new_land = scatter_total("kf", sl_ref, lslots) + ld_ref[...] * res_land
-    new_key = scatter_total("lm", sk_ref, kslots) + kd_ref[...] * res_key + win_ref[...]
-    new_land = new_land + beta * prod_land
-    new_key = new_key + beta * prod_key
-    part = inner(dir_land, new_land, dir_key, new_key)
-    tile = sum_all(two_rows(part, part), kf_more, lm_more, kft, lmt)
-    next_step = norm_next / tile[0:1, 0:1]
-    ol_ref[...] = step * old_land + next_step * dir_land
-    ok_ref[...] = step * old_key + next_step * dir_key
+    energy_next = tile[1:2, 0:1] + beta * (2.0 * tile[2:3, 0:1] + beta * energy)
+    next_step = norm_next / energy_next
+    ol_ref[...] = step * old_land + next_step * (res_land + beta * old_land)
+    ok_ref[...] = step * old_key + next_step * (res_key + beta * old_key)
 
 
 def exchange(kernel, identity, outs, scratch, *operands):
@@ -407,8 +433,9 @@
     tiles = [pltpu.VMEM((kf_count, 8, 128), F32), pltpu.VMEM((lm_count, 8, 128), F32)]
     sems = [kf_sems, lm_sems]
 
-    def seen(land_table, key_table):
-        land, key = observe(
+    def seen(spread, land_table, key_table):
+        return observe(
+            spread,
             live_blocks,
             land_table.reshape(-1, LOW),
             key_table.reshape(-1, LOW),
@@ -417,35 +444,34 @@
             land_pos,
             key_pos,
         )
-        return land.reshape(all_land), key.reshape(all_key)
 
     land_table, key_table = exchange(
         gather_kernel, 1, (all_land, all_key), sems, dir_land, dir_key
     )
     window = window_product(preint, dir_key)
-    sum_land, sum_key = seen(land_table, key_table)
+    sum_land, sum_key, squares = seen(True, land_table, key_table)
     res_land, res_key, own_res, prod_land, prod_key, scal = exchange(
         step_kernel,
         2,
         (all_land, all_key, own_key, own_land, own_key, (8, 128)),
         slots + tiles + sems * 3,
-        sum_land,
-        sum_key,
-        land_table,
-        key_table,
+        sum_land.reshape(all_land),
+        sum_key.reshape(all_key),
+        squares,
+        dir_land,
+        dir_key,
         damp_land,
         damp_key,
         window,
     )
     window = window_product(preint, own_res)
-    sum_land, sum_key = seen(res_land, res_key)
+    (squares,) = seen(False, res_land, res_key)
     sol_land, sol_key = exchange(
         last_kernel,
         3,
         (own_land, own_key),
-        slots + tiles * 2 + sems * 3,
-        sum_land,
-        sum_key,
+        tiles + sems,
+        squares,
         dir_land,
         dir_key,
         prod_land,

time: 107 us -> 79 us (0.74)
  Pallas kernels: 102 us -> 73.9 us
    pallas_call x2, Pallas kernels: 43.7 us -> 25.4 us  [observe(): pl.pallas_call(functools.partial(observe_kernel, spread), out_shape=tuple...]
    pallas_call x3, Pallas kernels: 47.8 us -> 38.1 us  [exchange(): pl.pallas_call(kernel, out_shape=tuple((jax.ShapeDtypeStruct(shape, F32)...]
where the time goes in v3:
time: 79 us; the launch traced here: 78.7 us
  Pallas kernels  73.9 us (94%)
  local copies, waits for them, and re-layouts  3.07 us (4%)
  between operations  1.66 us (2%)
    pallas_call x3, Pallas kernels, exchange(): pl.pallas_call(kernel, out_shape=tuple((jax.ShapeDtypeStruct(shape, F32)...  38.1 us
    pallas_call x2, Pallas kernels, observe(): pl.pallas_call(functools.partial(observe_kernel, spread), out_shape=tuple...  25.4 us
    pallas_call x2, Pallas kernels, window_product(): pl.pallas_call(window_kernel, out_shape=jax.ShapeDtypeStruct(direction.sh...  10.3 us
    reshape x4, local copies, waits for them, and re-layouts, fold_key(): parts = array.reshape(SDIM, states // LOW, LOW).transpose(1, 0, 2)  1.63 us

profile of v3, /device:TPU:0, one launch (start us, length us, event | category | flops | bytes accessed | tf_op | source)
XLA Modules:
  0.0 78.7 jit_solution(14003158911074833123)
XLA Ops:
  0.6 0.0 copy-start
  0.6 0.0 copy-start.1
  0.7 0.0 copy-start.5
  0.7 0.0 copy-start.2
  0.7 0.0 copy-start.4
  0.7 0.0 copy-start.3
  1.5 0.8 %reshape.50 = f32[15,2,256]{2,1,0:T(2,128)S(1)} reshape(f32[15,512]{1,0:T(8,128)} %param.11) | data formatting | bytes 61440 | tf_op jit(solution)/shard_map/reshape | solution.py:239
  2.4 0.8 reshape.57
  3.2 5.2 %shard_map.115.win_ref = f32[32,256]{1,0:T(8,128)S(1)} custom-call(f32[240,7680]{1,0:T(8,128)} %pre_ref.3, f32[32,256]{1,0:T(8,128)S(1)} %bitcast.22), custom_call_target="tpu_custom_call" | custom-call | tf_op jit(solution)/shard_map/pallas_call | solution.py:224
  8.3 0.0 copy-done.3
  8.4 0.0 copy-done.4
  8.5 0.0 copy-done.5
  8.5 0.1 fusion.2
  8.6 11.4 %shard_map.113 = (f32[4,48,256]{2,1,0:T(8,128)S(1)}, f32[8,32,256]{2,1,0:T(8,128)S(1)}) custom-call(f32[48,256]{1,0:T(8,128)S(1)} %reshape.49.land_ref.dl_ref, f32[32,256]{1,0:T(8,128)S(1)} %bitcast.23), custom_call_target="tpu_custom_call" | custom-call | tf_op jit(solution)/shard_map/pallas_call | solution.py:397
  19.9 0.0 copy-done
  20.0 0.0 copy-done.1
  20.0 0.0 copy-done.2
  20.0 16.6 %shard_map.114 = (f32[192,256]{1,0:T(8,128)S(1)}, f32[256,256]{1,0:T(8,128)S(1)}, f32[8,128]{1,0:T(8,128)S(1)}) custom-call(s32[1]{0:T(128)S(6)} %copy.20.live_ref, f32[192,256]{1,0:T(8,128)S(1)} %bitcast.37, f32[256,256]{1,0:T(8,128)S(1)} %bitcast.34, f32[6,16384]{1,0:T(8,128)S(1)} %copy-done.1, f32[30,16384]{1,0:T(8,128)S(1)} %copy-done, ...), custom_call_target="tpu_custom_call" | custom-call | tf_op jit(solution)/shard_map/pallas_call | solution.py:153
  36.6 18.1 %shard_map.116 = (f32[4,48,256]{2,1,0:T(8,128)S(1)}, f32[8,32,256]{2,1,0:T(8,128)S(1)}, f32[32,256]{1,0:T(8,128)S(1)}, f32[48,256]{1,0:T(8,128)S(1)}, f32[32,256]{1,0:T(8,128)S(1)}, /*index=5*/f32[8,128]{1,0:T(8,128)S(1)}) custom-call(f32[4,48,256]{2,1,0:T(8,128)S(1)} %bitcast.35, f32[8,32,256]{2,1,0:T(8,128)S(1)} %bitcast.32, ...), custom_call_target="tpu_custom_call" | custom-call | tf_op jit(solution)/shard_map/pallas_call | solution.py:397
  54.7 8.8 %shard_map.117.sq_ref = f32[8,128]{1,0:T(8,128)S(1)} custom-call(s32[1]{0:T(128)S(6)} %copy.20.live_ref, f32[192,256]{1,0:T(8,128)S(1)} %bitcast.36, f32[256,256]{1,0:T(8,128)S(1)} %bitcast.33, f32[6,16384]{1,0:T(8,128)S(1)} %copy-done.1, f32[30,16384]{1,0:T(8,128)S(1)} %copy-done, s32[1,16384]{1,0:T(1,128)S(1)} %bitcast.31, s32[1,16384]{1,0:T(1,128)S(1)} %bitcast.27), custom_call_target="tpu_custom_call" | custom-call | tf_op jit(solution)/shard_map/pallas_call | solution.py:153
  63.5 5.2 %shard_map.118.win_ref = f32[32,256]{1,0:T(8,128)S(1)} custom-call(f32[240,7680]{1,0:T(8,128)} %pre_ref.3, f32[32,256]{1,0:T(8,128)S(1)} %get-tuple-element.24.dir_ref), custom_call_target="tpu_custom_call" | custom-call | tf_op jit(solution)/shard_map/pallas_call | solution.py:224
  68.7 8.7 %shard_map.119 = (f32[48,256]{1,0:T(8,128)S(1)}, f32[32,256]{1,0:T(8,128)S(1)}) custom-call(f32[8,128]{1,0:T(8,128)S(1)} %shard_map.117.sq_ref, f32[48,256]{1,0:T(8,128)S(1)} %reshape.49.land_ref.dl_ref, f32[32,256]{1,0:T(8,128)S(1)} %bitcast.25, f32[48,256]{1,0:T(8,128)S(1)} %get-tuple-element.22.ql_ref, f32[32,256]{1,0:T(8,128)S(1)} %get-tuple-element.23.qk_ref, ...), custom_call_target="tpu_custom_call" | custom-call | tf_op jit(solution)/shard_map/pallas_call | solution.py:397
  77.5 0.6 copy.15
  78.1 0.7 reshape.61
  (9 shorter events, 0.1 us)
Async XLA Ops:
  0.6 19.3 %copy-start = (f32[30,16384]{1,0:T(8,128)S(1)}, f32[30,16384]{1,0:T(8,128)}, u32[]{:S(2)}) copy-start(f32[30,16384]{1,0:T(8,128)} %kj_ref.3) | copy-start | bytes 5898244
  0.6 19.3 %copy-start.1 = (f32[6,16384]{1,0:T(8,128)S(1)}, f32[6,16384]{1,0:T(8,128)}, u32[]{:S(2)}) copy-start(f32[6,16384]{1,0:T(8,128)} %lj_ref.3) | copy-start | bytes 1179652
  0.7 7.8 %copy-start.5 = (s32[16384]{0:T(1024)S(1)}, s32[16384]{0:T(1024)}, u32[]{:S(2)}) copy-start(s32[16384]{0:T(1024)} %param.17) | copy-start | bytes 196612
  0.7 19.3 %copy-start.2 = (s32[16384]{0:T(1024)S(1)}, s32[16384]{0:T(1024)}, u32[]{:S(2)}) copy-start(s32[16384]{0:T(1024)} %param.16) | copy-start | bytes 196612
  0.7 7.7 %copy-start.4 = (f32[3,4096]{1,0:T(4,128)S(1)}, f32[3,4096]{1,0:T(4,128)}, u32[]{:S(2)}) copy-start(f32[3,4096]{1,0:T(4,128)} %param.12) | copy-start | bytes 147460
  0.7 7.7 %copy-start.3 = (f32[3,4096]{1,0:T(4,128)S(1)}, f32[3,4096]{1,0:T(4,128)}, u32[]{:S(2)}) copy-start(f32[3,4096]{1,0:T(4,128)} %param.10) | copy-start | bytes 147460
